TPU v7x, 128 devices: a whole 4x4x4 slice. The times are simulated.
128 devices in a mesh: hst: 16 (over z, x), doc: 8 (over y, core).
Axes of the slice: x: 4, y: 4, z: 4, core: 2. Of those that a mesh axis runs over, the one named last changes fastest.
Arguments:
- docs: bfloat16 [1048576, 768], P(('hst', 'doc')), may hold values from -400 to 400, as said below
- w_in: bfloat16 [768, 256], replicated, may hold values from -0.21875 to 0.21875
- w_out: bfloat16 [256, 64], replicated, may hold values from -0.375 to 0.375
- doc_host: int32 [1048576], P(('hst', 'doc')), may hold values from 0 to 2047
- tiles: bfloat16 [8192, 128, 128], P(('hst', 'doc')), may hold values from 0 to 10, as said below
- dst_block: int32 [8192], P(('hst', 'doc')), may hold values from 0 to 15
- src_block: int32 [8192], P(('hst', 'doc')), may hold values from 0 to 255
- tile_count: int32 [128], P(('hst', 'doc')), may hold values from 1 to 64, as said below
- teleport: int32 [32768], P('hst'), may hold values 0 or 1
Outputs:
- scores: float32 [32768, 64], P(('hst', 'doc'))
Inputs may be any that keep to these rules, and one draw needn't show every extreme that they name: `docs`: embeddings stay in the stated range. `tiles`: link weights are nonnegative. `tile_count`: some device uses all 64 slots.
All inputs are finite; a program needn't handle non-finite values. No bound on the sum of `teleport` on one device may be relied on, other than what follows from the above.
Results may differ from a plain program's by a relative error of at most 0.00066.
Values may be sent and summed in bfloat16 or wider, within the bound.
A program may use at most 128 MiB of HBM per device.

v0:
```python
import jax
import jax.numpy as jnp
from jax import lax
from jax.sharding import PartitionSpec as P

HOPS = 3


def body(docs, w_in, w_out, doc_host, tiles, dst_block, src_block, tile_count, teleport):
    host_dev = teleport.shape[0]
    block = tiles.shape[1]
    topics = w_out.shape[1]
    slots = tiles.shape[0]
    hosts_all = host_dev * lax.axis_size("hst")
    nblocks = hosts_all // block
    hidden = jax.nn.gelu(
        jnp.dot(docs, w_in, preferred_element_type=jnp.float32), approximate=True
    ).astype(jnp.bfloat16)
    probs = jax.nn.softmax(jnp.dot(hidden, w_out, preferred_element_type=jnp.float32), axis=-1)
    local_topic = jax.ops.segment_sum(probs, doc_host, num_segments=host_dev)
    used = (jnp.arange(slots) < tile_count[0]).astype(jnp.float32)
    colsum = jnp.sum(tiles, axis=1, dtype=jnp.float32)
    src_onehot = (src_block[:, None] == jnp.arange(nblocks)[None, :]).astype(jnp.float32) * used[
        :, None
    ]
    degree_blocks = jnp.dot(src_onehot.T, colsum, precision=lax.Precision.HIGHEST)
    degree = lax.psum(degree_blocks, ("hst", "doc")).reshape(hosts_all)
    own_degree = lax.dynamic_slice_in_dim(degree, lax.axis_index("hst") * host_dev, host_dev)
    inverse = 1.0 / jnp.maximum(own_degree, 1.0)
    dst_onehot = (dst_block[:, None] == jnp.arange(host_dev // block)[None, :]).astype(
        jnp.float32
    ) * used[:, None]
    member = teleport.astype(jnp.float32)
    rows = host_dev // lax.axis_size("doc")
    host_topic = lax.psum(local_topic, "doc")
    mass = lax.psum(jnp.sum(member[:, None] * host_topic, axis=0), "hst")
    tele = member[:, None] * host_topic / mass
    state = tele
    for hop in range(HOPS):
        sent = (state * inverse[:, None]).astype(jnp.bfloat16)
        full = lax.all_gather(sent, "hst", axis=0, tiled=True)
        slabs = full.reshape(nblocks, block, topics)[src_block]
        prod = jnp.einsum("kij,kjt->kit", tiles, slabs, preferred_element_type=jnp.float32)
        gathered = jnp.einsum("kb,kit->bit", dst_onehot, prod, precision=lax.Precision.HIGHEST)
        inflow = lax.psum(gathered.reshape(host_dev, topics), "doc")
        state = 0.85 * inflow + 0.15 * tele
    result = lax.dynamic_slice_in_dim(state, lax.axis_index("doc") * rows, rows)
    return hosts_all * result


def solution(mesh):
    placed = (
        P(("hst", "doc"), None),
        P(),
        P(),
        P(("hst", "doc")),
        P(("hst", "doc"), None, None),
        P(("hst", "doc")),
        P(("hst", "doc")),
        P(("hst", "doc")),
        P("hst"),
    )
    return jax.shard_map(
        body, mesh=mesh, in_specs=placed, out_specs=P(("hst", "doc"), None), check_vma=False
    )
```

profile of v0, /device:TPU:0, one launch (start us, length us, event | category | flops | bytes accessed | tf_op | source)
XLA Modules:
  0.0 640.4 jit_solution(17008999515403632906)
XLA Ops:
  6.5 0.0 copy-start
  7.3 2.1 convert_reduce_fusion
  9.4 0.0 copy-done.5
  9.4 1.8 convolution_bitcast_fusion
  11.1 0.0 all-reduce.8.cloned.1.call-update
  11.2 0.0 all-reduce.6.cloned.1.call-start
  11.2 8.6 %fusion.48 = (f32[8192]{0:T(1024)S(1)}, f32[8192,64]{0,1:T(8,128)S(1)}) fusion(bf16[256,64]{0,1:T(8,128)(2,1)} %param.11, bf16[8192,768]{1,0:T(8,128)(2,1)} %param.9, bf16[768,256]{1,0:T(8,128)(2,1)S(1)} %copy-done), kind=kOutput, calls=%fused_computation.78 | convolution fusion | flops 3509051392 | bytes 15138816 | tf_op jit(solution)/shard_map/dot_general | solution.py:19
  19.9 1.3 copy-done.2
  21.2 0.3 fusion.17
  21.6 1.9 fusion.16
  23.5 0.0 copy-start.8
  23.5 0.0 copy-start.13
  23.5 2.7 copy.18
  26.2 44.5 %scatter_custom_fusion = f32[2048,64]{1,0:T(8,128)S(1)} fusion(s32[8192]{0:T(1024)} %param.12, f32[8192,64]{1,0:T(8,128)} %copy.18, f32[]{:T(128)} %constant.16.clone.1), kind=kCustom, calls=%fused_computation.37 | custom fusion | flops 524288 | bytes 524800 | tf_op jit(solution)/shard_map/scatter-add | solution.py:20
  70.8 1.1 copy.19
  71.9 0.0 all-reduce.6.cloned.1.call-update
  71.9 0.0 all-gather.4.cloned.1.call-start
  72.0 82.8 %all-reduce.8.cloned.1.call-done = f32[32768]{0:T(1024)} async-done(((f32[32768]{0:T(1024)}), f32[32768]{0:T(1024)}) %all-reduce.8.cloned.1.call-update) | async-done | bytes 131088 | tf_op jit(solution)/shard_map/psum | solution.py:27
  154.8 0.7 maximum_divide_fusion
  155.5 59.7 %all-reduce.6.cloned.1.call-done = f32[2048,64]{0,1:T(8,128)} async-done(((f32[2048,64]{0,1:T(8,128)}), f32[2048,64]{0,1:T(8,128)}) %all-reduce.6.cloned.1.call-update) | async-done | bytes 524304 | tf_op jit(solution)/shard_map/psum | solution.py:35
  215.2 1.2 multiply_reduce_fusion
  216.4 40.5 %psum.43 = f32[64]{0:T(128)S(1)} all-reduce(f32[64]{0:T(128)S(1)} %multiply_reduce_fusion), channel_id=1, replica_groups=mesh['hst'=16,'doc'=8] {'hst'}, use_global_device_ids=true, to_apply=%region_5.0 | all-reduce | flops 64 | bytes 512 | tf_op jit(solution)/shard_map/psum | solution.py:36
  256.9 1.9 multiply_convert_fusion.2
  258.8 0.0 all-gather.4.cloned.1.call-update
  258.8 0.2 all-reduce.10.cloned.1.call-start
  259.1 0.6 pad_clamp_fusion
  259.7 44.7 %all-gather.4.cloned.1.call-done = bf16[32768,64]{0,1:T(8,128)(2,1)} async-done(((bf16[2048,64]{0,1:T(8,128)(2,1)}), bf16[32768,64]{0,1:T(8,128)(2,1)}) %all-gather.4.cloned.1.call-update) | async-done | bytes 4194320 | tf_op jit(solution)/shard_map/all_gather | solution.py:41
  304.4 0.0 copy-done.11
  304.4 5.4 copy_bitcast_fusion.2
  309.8 3.2 gather_fusion
  313.0 0.0 copy-start.9
  313.0 1.5 convolution_bitcast_fusion.3
  314.5 0.0 copy-done.9
  314.6 2.2 fusion.14
  316.8 1.0 copy.46
  317.8 0.0 all-reduce.10.cloned.1.call-update
  317.8 0.0 all-gather.6.cloned.1.call-start
  317.8 60.4 %all-reduce.10.cloned.1.call-done = f32[2048,64]{0,1:T(8,128)} async-done(((f32[2048,64]{0,1:T(8,128)}), f32[2048,64]{0,1:T(8,128)}) %all-reduce.10.cloned.1.call-update) | async-done | bytes 524304 | tf_op jit(solution)/shard_map/psum | solution.py:45
  378.3 0.0 copy-done.3
  378.3 2.2 multiply_convert_fusion.1
  380.5 0.0 all-gather.6.cloned.1.call-update
  380.5 0.0 all-reduce.12.cloned.1.call-start
  380.6 51.0 %all-gather.6.cloned.1.call-done = bf16[32768,64]{0,1:T(8,128)(2,1)} async-done(((bf16[2048,64]{0,1:T(8,128)(2,1)}), bf16[32768,64]{0,1:T(8,128)(2,1)}) %all-gather.6.cloned.1.call-update) | async-done | bytes 4194320 | tf_op jit(solution)/shard_map/all_gather | solution.py:41
  431.6 5.4 copy_bitcast_fusion.1
  436.9 3.1 gather_fusion.1
  440.0 1.5 convolution_bitcast_fusion.2
  441.6 0.0 copy-done.10
  441.6 2.2 fusion.12
  443.8 1.0 copy.45
  444.8 0.0 all-reduce.12.cloned.1.call-update
  444.8 0.0 all-gather.8.cloned.1.call-start
  444.8 60.4 %all-reduce.12.cloned.1.call-done = f32[2048,64]{0,1:T(8,128)} async-done(((f32[2048,64]{0,1:T(8,128)}), f32[2048,64]{0,1:T(8,128)}) %all-reduce.12.cloned.1.call-update) | async-done | bytes 524304 | tf_op jit(solution)/shard_map/psum | solution.py:45
  505.3 1.8 multiply_convert_fusion
  507.1 0.0 all-gather.8.cloned.1.call-update
  507.1 0.3 all-reduce.14.cloned.1.call-start
  507.4 51.0 %all-gather.8.cloned.1.call-done = bf16[32768,64]{0,1:T(8,128)(2,1)} async-done(((bf16[2048,64]{0,1:T(8,128)(2,1)}), bf16[32768,64]{0,1:T(8,128)(2,1)}) %all-gather.8.cloned.1.call-update) | async-done | bytes 4194320 | tf_op jit(solution)/shard_map/all_gather | solution.py:41
  558.4 5.4 copy_bitcast_fusion
  563.7 3.1 gather_fusion.2
  566.8 1.5 convolution_bitcast_fusion.1
  568.3 2.2 fusion.10
  570.6 1.0 copy.44
  571.5 0.0 all-reduce.14.cloned.1.call-update
  571.6 60.5 %all-reduce.14.cloned.1.call-done = f32[2048,64]{0,1:T(8,128)} async-done(((f32[2048,64]{0,1:T(8,128)}), f32[2048,64]{0,1:T(8,128)}) %all-reduce.14.cloned.1.call-update) | async-done | bytes 524304 | tf_op jit(solution)/shard_map/psum | solution.py:45
  632.0 1.5 fusion.20
  (22 shorter events, 0.0 us)
Async XLA Ops:
  6.5 4.7 copy-start
  6.5 148.3 %all-reduce.8.cloned.1.call-start = ((), (), s32[]{:S(2)}) async-start(), calls=%async_computation.1 | async-start | bytes 262144 | tf_op jit(solution)/shard_map/psum | solution.py:27
  7.3 2.1 copy-start.5
  11.2 204.0 %all-reduce.6.cloned.1.call-start = ((), (), s32[]{:S(2)}) async-start(), calls=%async_computation | async-start | bytes 1048576 | tf_op jit(solution)/shard_map/psum | solution.py:35
  19.9 1.3 copy-start.2
  23.5 48.5 %copy-start.8 = (s32[2048]{0:T(1024)S(1)}, s32[2048]{0:T(1024)}, u32[]{:S(2)}) copy-start(s32[2048]{0:T(1024)} %param.17) | copy-start | bytes 24580
  23.5 235.5 %copy-start.13 = (s32[64]{0:T(128)S(1)}, s32[64]{0:T(128)}, u32[]{:S(2)}) copy-start(s32[64]{0:T(128)} %param.15) | copy-start | bytes 772
  71.9 232.4 %all-gather.4.cloned.1.call-start = ((), (), s32[]{:S(2)}) async-start(), calls=%async_computation.2 | async-start | bytes 4456448 | tf_op jit(solution)/shard_map/all_gather | solution.py:41
  256.9 47.5 %copy-start.11 = (f32[64]{0:T(128)}, f32[64]{0:T(128)S(1)}, u32[]{:S(2)}) copy-start(f32[64]{0:T(128)S(1)} %psum.43) | copy-start | bytes 772
  258.8 119.5 %all-reduce.10.cloned.1.call-start = ((), (), s32[]{:S(2)}) async-start(), calls=%async_computation.3 | async-start | bytes 1048576 | tf_op jit(solution)/shard_map/psum | solution.py:45
  309.8 3.2 copy-start.1
  313.0 1.6 copy-start.6
  313.0 1.6 copy-start.9
  314.6 63.7 %copy-start.3 = (f32[2048,64]{0,1:T(8,128)S(1)}, f32[2048,64]{0,1:T(8,128)}, u32[]{:S(2)}) copy-start(f32[2048,64]{0,1:T(8,128)} %all-reduce.6.cloned.1.call-done) | copy-start | bytes 1572868
  314.6 63.7 %copy-start.12 = (f32[64]{0:T(128)S(1)}, f32[64]{0:T(128)}, u32[]{:S(2)}) copy-start(f32[64]{0:T(128)} %copy-done.11) | copy-start | bytes 772
  317.8 113.8 %all-gather.6.cloned.1.call-start = ((), (), s32[]{:S(2)}) async-start(), calls=%async_computation.4 | async-start | bytes 4456448 | tf_op jit(solution)/shard_map/all_gather | solution.py:41
  380.5 124.8 %all-reduce.12.cloned.1.call-start = ((), (), s32[]{:S(2)}) async-start(), calls=%async_computation.5 | async-start | bytes 1048576 | tf_op jit(solution)/shard_map/psum | solution.py:45
  436.9 4.6 copy-start.7
  436.9 4.6 copy-start.10
  441.6 63.7 %copy-start.4 = (f32[2048,64]{0,1:T(8,128)S(1)}, f32[2048,64]{0,1:T(8,128)}, u32[]{:S(2)}) copy-start(f32[2048,64]{0,1:T(8,128)} %get-tuple-element.6) | copy-start | bytes 1572868
  444.8 113.6 %all-gather.8.cloned.1.call-start = ((), (), s32[]{:S(2)}) async-start(), calls=%async_computation.6 | async-start | bytes 4456448 | tf_op jit(solution)/shard_map/all_gather | solution.py:41
  507.1 124.9 %all-reduce.14.cloned.1.call-start = ((), (), s32[]{:S(2)}) async-start(), calls=%async_computation.7 | async-start | bytes 1048576 | tf_op jit(solution)/shard_map/psum | solution.py:45
Sparse Core Ops, SparseCore 0:
  12.1 142.6 all-reduce.7
  157.2 57.9 all-reduce.5
  258.9 45.3 all-gather.3
  317.9 60.3 all-reduce.9
  380.6 50.8 all-gather.5
  444.9 60.3 all-reduce.11
  507.4 50.8 all-gather.7
  571.7 60.3 all-reduce.13
where the time goes:
time: 641 us; the launch traced here: 640 us
  waiting for transfers between devices  471 us (73%)
  other arithmetic  58.8 us (9%)
  blocking collectives  40.5 us (6%)
  local copies, waits for them, and re-layouts  33.6 us (5%)
  matrix products  21.7 us (3%)
  between operations  14.4 us (2%)
    psum x3, waiting for transfers between devices, body(): inflow = lax.psum(gathered.reshape(host_dev, topics), 'doc')  181 us
    all_gather x3, waiting for transfers between devices, body(): full = lax.all_gather(sent, 'hst', axis=0, tiled=True)  147 us
    psum x1, waiting for transfers between devices, body(): degree = lax.psum(degree_blocks, ('hst', 'doc')).reshape(hosts_all)  82.8 us
    psum x1, waiting for transfers between devices, body(): host_topic = lax.psum(local_topic, 'doc')  59.7 us
    scatter-add x1, other arithmetic, body(): local_topic = jax.ops.segment_sum(probs, doc_host, num_segments=host_dev)  44.5 us
    psum x1, blocking collectives, body(): mass = lax.psum(jnp.sum(member[:, None] * host_topic, axis=0), 'hst')  40.5 us
    reshape x3, local copies, waits for them, and re-layouts, body(): slabs = full.reshape(nblocks, block, topics)[src_block]  16.1 us
  transfers between devices with their start and end apart: 8, of which 8 were waited for; matrix products, arithmetic and copies ran while one was open for 9% of the time, Pallas kernels for 0%

commit v1 on v0

--- a/solution.py
+++ b/solution.py
@@ -33,7 +33,7 @@
     member = teleport.astype(jnp.float32)
     rows = host_dev // lax.axis_size("doc")
     host_topic = lax.psum(local_topic, "doc")
-    mass = lax.psum(jnp.sum(member[:, None] * host_topic, axis=0), "hst")
+    mass = jnp.sum(lax.all_gather(jnp.sum(member[:, None] * host_topic, axis=0), "hst"), axis=0)
     tele = member[:, None] * host_topic / mass
     state = tele
     for hop in range(HOPS):

time: 641 us -> 641 us (level)
    psum x1 -> x0, blocking collectives: 40.5 us -> none  [body(): mass = lax.psum(jnp.sum(member[:, None] * host_topic, axis=0), 'hst')]
    unnamed x0 -> x1, blocking collectives: none -> 40.5 us
  transfers between devices with their start and end apart: 8 -> 8, of which waited for: 8 -> 8; matrix products, arithmetic and copies ran while one was open for 9% -> 10% of each run, Pallas kernels for 0% -> 0%
where the time goes in v1:
time: 641 us
  waiting for transfers between devices  469 us (73%)
  other arithmetic  58.8 us (9%)
  blocking collectives  40.5 us (6%)
  local copies, waits for them, and re-layouts  34.5 us (5%)
  matrix products  21.7 us (3%)
  between operations  15.1 us (2%)
    psum x3, waiting for transfers between devices, body(): inflow = lax.psum(gathered.reshape(host_dev, topics), 'doc')  181 us
    all_gather x3, waiting for transfers between devices, body(): full = lax.all_gather(sent, 'hst', axis=0, tiled=True)  147 us
    psum x1, waiting for transfers between devices, body(): degree = lax.psum(degree_blocks, ('hst', 'doc')).reshape(hosts_all)  81.6 us
    psum x1, waiting for transfers between devices, body(): host_topic = lax.psum(local_topic, 'doc')  59.7 us
    scatter-add x1, other arithmetic, body(): local_topic = jax.ops.segment_sum(probs, doc_host, num_segments=host_dev)  44.5 us
    unnamed x1, blocking collectives  40.5 us
    reshape x3, local copies, waits for them, and re-layouts, body(): slabs = full.reshape(nblocks, block, topics)[src_block]  16.1 us
  transfers between devices with their start and end apart: 8, of which 8 were waited for; matrix products, arithmetic and copies ran while one was open for 10% of the time, Pallas kernels for 0%

profile of v1, /device:TPU:0, one launch (start us, length us, event | category | flops | bytes accessed | tf_op | source)
XLA Modules:
  0.0 640.7 jit_solution(10580137177298257321)
XLA Ops:
  7.3 2.1 convert_reduce_fusion
  9.4 1.8 convolution_bitcast_fusion
  11.1 0.0 all-reduce.9.cloned.1.call-update
  11.2 0.0 all-reduce.7.cloned.1.call-start
  11.2 8.6 %fusion.48 = (f32[8192]{0:T(1024)S(1)}, f32[8192,64]{0,1:T(8,128)S(1)}) fusion(bf16[256,64]{0,1:T(8,128)(2,1)} %param.11, bf16[8192,768]{1,0:T(8,128)(2,1)} %param.9, bf16[768,256]{1,0:T(8,128)(2,1)S(1)} %copy-done), kind=kOutput, calls=%fused_computation.78 | convolution fusion | flops 3509051392 | bytes 15138816 | tf_op jit(solution)/shard_map/dot_general | solution.py:19
  19.9 1.3 copy-done.2
  21.2 0.3 fusion.17
  21.5 1.9 fusion.16
  23.5 0.0 copy-start.8
  23.5 0.0 copy-start.14
  23.5 0.0 copy-start.13
  23.5 2.7 copy.29
  26.2 44.5 %scatter_custom_fusion = f32[2048,64]{1,0:T(8,128)S(1)} fusion(s32[8192]{0:T(1024)} %param.12, f32[8192,64]{1,0:T(8,128)} %copy.29, f32[]{:T(128)} %constant.16.clone.1), kind=kCustom, calls=%fused_computation.37 | custom fusion | flops 524288 | bytes 524800 | tf_op jit(solution)/shard_map/scatter-add | solution.py:20
  70.8 1.1 copy.30
  71.9 0.0 all-reduce.7.cloned.1.call-update
  71.9 0.0 all-gather.5.cloned.1.call-start
  72.0 0.6 dynamic-slice
  73.2 81.6 %all-reduce.9.cloned.1.call-done = f32[32768]{0:T(1024)} async-done(((f32[32768]{0:T(1024)}), f32[32768]{0:T(1024)}) %all-reduce.9.cloned.1.call-update) | async-done | bytes 131088 | tf_op jit(solution)/shard_map/psum | solution.py:27
  154.8 0.7 maximum_divide_fusion
  155.5 59.7 %all-reduce.7.cloned.1.call-done = f32[2048,64]{0,1:T(8,128)} async-done(((f32[2048,64]{0,1:T(8,128)}), f32[2048,64]{0,1:T(8,128)}) %all-reduce.7.cloned.1.call-update) | async-done | bytes 524304 | tf_op jit(solution)/shard_map/psum | solution.py:35
  215.2 1.2 multiply_reduce_fusion
  216.4 0.2 dynamic-update-slice
  216.7 40.5 %all-reduce = f32[1024]{0:T(1024)S(1)} all-reduce(f32[1024]{0:T(1024)S(1)} %dynamic-update-slice), channel_id=2, replica_groups=mesh['hst'=16,'doc'=8] {'hst'}, use_global_device_ids=true, to_apply=%add | all-reduce | flops 1024 | bytes 8192
  257.2 0.1 reshape.72
  257.3 1.9 multiply_convert_fusion.2
  259.1 0.0 all-gather.5.cloned.1.call-update
  259.1 0.2 all-reduce.11.cloned.1.call-start
  259.4 0.6 pad_clamp_fusion
  260.0 44.7 %all-gather.5.cloned.1.call-done = bf16[32768,64]{0,1:T(8,128)(2,1)} async-done(((bf16[2048,64]{0,1:T(8,128)(2,1)}), bf16[32768,64]{0,1:T(8,128)(2,1)}) %all-gather.5.cloned.1.call-update) | async-done | bytes 4194320 | tf_op jit(solution)/shard_map/all_gather | solution.py:41
  304.7 5.4 copy_bitcast_fusion.2
  310.1 3.2 gather_fusion
  313.3 0.0 copy-start.9
  313.3 1.5 convolution_bitcast_fusion.3
  314.9 0.0 copy-done.9
  314.9 2.2 fusion.14
  317.1 1.0 copy.57
  318.1 0.0 all-reduce.11.cloned.1.call-update
  318.1 0.0 all-gather.7.cloned.1.call-start
  318.2 60.5 %all-reduce.11.cloned.1.call-done = f32[2048,64]{0,1:T(8,128)} async-done(((f32[2048,64]{0,1:T(8,128)}), f32[2048,64]{0,1:T(8,128)}) %all-reduce.11.cloned.1.call-update) | async-done | bytes 524304 | tf_op jit(solution)/shard_map/psum | solution.py:45
  378.6 2.2 multiply_convert_fusion.1
  380.8 0.0 all-gather.7.cloned.1.call-update
  380.8 0.0 all-reduce.13.cloned.1.call-start
  380.9 51.0 %all-gather.7.cloned.1.call-done = bf16[32768,64]{0,1:T(8,128)(2,1)} async-done(((bf16[2048,64]{0,1:T(8,128)(2,1)}), bf16[32768,64]{0,1:T(8,128)(2,1)}) %all-gather.7.cloned.1.call-update) | async-done | bytes 4194320 | tf_op jit(solution)/shard_map/all_gather | solution.py:41
  431.9 5.4 copy_bitcast_fusion.1
  437.3 3.1 gather_fusion.1
  440.3 1.5 convolution_bitcast_fusion.2
  441.9 0.0 copy-done.10
  441.9 2.2 fusion.12
  444.1 1.0 copy.56
  445.1 0.0 all-reduce.13.cloned.1.call-update
  445.1 0.0 all-gather.9.cloned.1.call-start
  445.2 60.4 %all-reduce.13.cloned.1.call-done = f32[2048,64]{0,1:T(8,128)} async-done(((f32[2048,64]{0,1:T(8,128)}), f32[2048,64]{0,1:T(8,128)}) %all-reduce.13.cloned.1.call-update) | async-done | bytes 524304 | tf_op jit(solution)/shard_map/psum | solution.py:45
  505.6 1.8 multiply_convert_fusion
  507.4 0.0 all-gather.9.cloned.1.call-update
  507.4 0.3 all-reduce.15.cloned.1.call-start
  507.7 51.0 %all-gather.9.cloned.1.call-done = bf16[32768,64]{0,1:T(8,128)(2,1)} async-done(((bf16[2048,64]{0,1:T(8,128)(2,1)}), bf16[32768,64]{0,1:T(8,128)(2,1)}) %all-gather.9.cloned.1.call-update) | async-done | bytes 4194320 | tf_op jit(solution)/shard_map/all_gather | solution.py:41
  558.7 5.4 copy_bitcast_fusion
  564.0 3.1 gather_fusion.2
  567.1 1.5 convolution_bitcast_fusion.1
  568.6 2.2 fusion.10
  570.9 1.0 copy.55
  571.8 0.0 all-reduce.15.cloned.1.call-update
  571.9 60.5 %all-reduce.15.cloned.1.call-done = f32[2048,64]{0,1:T(8,128)} async-done(((f32[2048,64]{0,1:T(8,128)}), f32[2048,64]{0,1:T(8,128)}) %all-reduce.15.cloned.1.call-update) | async-done | bytes 524304 | tf_op jit(solution)/shard_map/psum | solution.py:45
  632.4 1.5 fusion.20
  (29 shorter events, 0.1 us)
Async XLA Ops:
  6.5 4.7 copy-start
  6.5 148.3 %all-reduce.9.cloned.1.call-start = ((), (), s32[]{:S(2)}) async-start(), calls=%async_computation.1 | async-start | bytes 262144 | tf_op jit(solution)/shard_map/psum | solution.py:27
  7.3 2.1 copy-start.5
  11.2 204.0 %all-reduce.7.cloned.1.call-start = ((), (), s32[]{:S(2)}) async-start(), calls=%async_computation | async-start | bytes 1048576 | tf_op jit(solution)/shard_map/psum | solution.py:35
  19.9 1.3 copy-start.2
  23.5 48.5 %copy-start.8 = (s32[2048]{0:T(1024)S(1)}, s32[2048]{0:T(1024)}, u32[]{:S(2)}) copy-start(s32[2048]{0:T(1024)} %param.17) | copy-start | bytes 24580
  23.5 48.5 %copy-start.14 = (u32[128]{0:T(128)S(1)}, u32[128]{0:T(128)}, u32[]{:S(2)}) copy-start(u32[128]{0:T(128)} %constant.48) | copy-start | bytes 1540
  23.5 235.9 %copy-start.13 = (s32[64]{0:T(128)S(1)}, s32[64]{0:T(128)}, u32[]{:S(2)}) copy-start(s32[64]{0:T(128)} %param.15) | copy-start | bytes 772
  71.9 232.8 %all-gather.5.cloned.1.call-start = ((), (), s32[]{:S(2)}) async-start(), calls=%async_computation.2 | async-start | bytes 4456448 | tf_op jit(solution)/shard_map/all_gather | solution.py:41
  257.3 47.5 %copy-start.11 = (f32[64]{0:T(128)}, f32[64]{0:T(128)S(1)}, u32[]{:S(2)}) copy-start(f32[64]{0:T(128)S(1)} %reduce_sum.38) | copy-start | bytes 772
  259.1 119.5 %all-reduce.11.cloned.1.call-start = ((), (), s32[]{:S(2)}) async-start(), calls=%async_computation.3 | async-start | bytes 1048576 | tf_op jit(solution)/shard_map/psum | solution.py:45
  310.1 3.2 copy-start.1
  313.3 1.6 copy-start.6
  313.3 1.6 copy-start.9
  314.9 63.8 %copy-start.3 = (f32[2048,64]{0,1:T(8,128)S(1)}, f32[2048,64]{0,1:T(8,128)}, u32[]{:S(2)}) copy-start(f32[2048,64]{0,1:T(8,128)} %all-reduce.7.cloned.1.call-done) | copy-start | bytes 1572868
  314.9 63.8 %copy-start.12 = (f32[64]{0:T(128)S(1)}, f32[64]{0:T(128)}, u32[]{:S(2)}) copy-start(f32[64]{0:T(128)} %copy-done.11) | copy-start | bytes 772
  318.1 113.8 %all-gather.7.cloned.1.call-start = ((), (), s32[]{:S(2)}) async-start(), calls=%async_computation.4 | async-start | bytes 4456448 | tf_op jit(solution)/shard_map/all_gather | solution.py:41
  380.8 124.8 %all-reduce.13.cloned.1.call-start = ((), (), s32[]{:S(2)}) async-start(), calls=%async_computation.5 | async-start | bytes 1048576 | tf_op jit(solution)/shard_map/psum | solution.py:45
  437.3 4.6 copy-start.7
  437.3 4.6 copy-start.10
  441.9 63.7 %copy-start.4 = (f32[2048,64]{0,1:T(8,128)S(1)}, f32[2048,64]{0,1:T(8,128)}, u32[]{:S(2)}) copy-start(f32[2048,64]{0,1:T(8,128)} %get-tuple-element.6) | copy-start | bytes 1572868
  445.1 113.6 %all-gather.9.cloned.1.call-start = ((), (), s32[]{:S(2)}) async-start(), calls=%async_computation.6 | async-start | bytes 4456448 | tf_op jit(solution)/shard_map/all_gather | solution.py:41
  507.4 125.0 %all-reduce.15.cloned.1.call-start = ((), (), s32[]{:S(2)}) async-start(), calls=%async_computation.7 | async-start | bytes 1048576 | tf_op jit(solution)/shard_map/psum | solution.py:45
Sparse Core Ops, SparseCore 0:
  12.1 142.6 all-reduce.8
  157.2 57.9 all-reduce.6
  259.3 45.3 all-gather.4
  318.2 60.3 all-reduce.10
  381.0 50.8 all-gather.6
  445.2 60.3 all-reduce.12
  507.7 50.8 all-gather.8
  572.0 60.3 all-reduce.14
